TPU v7x, 256 devices: a whole 4x4x8 slice. The times are simulated.
256 devices in a mesh: dp: 8 (over x, z_lo), expert: 32 (over y, z_hi, core).
Axes of the slice: x: 4, y: 4, z: 8 (z_hi: 4, z_lo: 2; z = z_hi * 2 + z_lo), core: 2. Of those that a mesh axis runs over, the one named last changes fastest.
Arguments:
- tokens: bfloat16 [32768, 1664], P(('dp', 'expert')), may hold values from -6 to 6
- cotangent: bfloat16 [32768, 1664], P(('dp', 'expert')), may hold values from -6 to 6
- expert_idx: int32 [32768, 2], P(('dp', 'expert')), may hold values from 0 to 31, as said below
- expert_slot: int32 [32768, 2], P(('dp', 'expert')), may hold values from -1 to 5, as said below
- combine: float32 [32768, 2], P(('dp', 'expert')), may hold values from 0.2 to 1
- gain: float32 [1664], replicated, may hold values from 0.5 to 1.5
- shift: float32 [1664], replicated, may hold values from -3 to 3
- w_in: bfloat16 [32, 1664, 4096], P('expert', None, 'dp'), may hold values from -0.15625 to 0.15625
- b_in: float32 [32, 4096], P('expert', 'dp'), may hold values from -3 to 3
- w_out: bfloat16 [32, 4096, 1664], P('expert', 'dp'), may hold values from -0.09375 to 0.09375
Outputs:
- grad_tokens: bfloat16 [32768, 1664], P(('dp', 'expert'))
- grad_w_in: float32 [32, 1664, 4096], P('expert', None, 'dp')
- grad_b_in: float32 [32, 4096], P('expert', 'dp')
- grad_w_out: float32 [32, 4096, 1664], P('expert', 'dp')
- gain_gradient: float32 [1664], replicated
- grad_shift: float32 [1664], replicated
Inputs may be any that keep to these rules, and one draw needn't show every extreme that they name: `expert_idx`: an expert number of 0 to 31; the two choices of a patch differ. `expert_slot`: within the 128 patches of one device, the live slots of one expert are 0, 1, ... without repeats, at most 6 of them; -1 marks a dropped choice.
All inputs are finite; a program needn't handle non-finite values.
Results may differ from a plain program's by a relative error of at most 0.018.
Values may be sent and summed in bfloat16 or wider, within the bound.
No kernel may reach another device: no remote copies, remote signals or barrier semaphores. Data moves between devices by JAX's collectives and lax.ppermute only.
A program may use at most 128 MiB of HBM per device.

v0:
```python
import functools
import math

import jax
import jax.numpy as jnp
import numpy as np
from jax import lax
from jax.experimental import pallas as pl
from jax.experimental.pallas import tpu as pltpu
from jax.sharding import PartitionSpec as P

inv_root_two = 1.0 / math.sqrt(2.0)
inv_root_tau = 1.0 / math.sqrt(2.0 * math.pi)
f32, bf16 = jnp.float32, jnp.bfloat16

RIGHT = [(i, (i + 2) % 8) for i in range(8)]
LEFT = [(i, (i - 2) % 8) for i in range(8)]
ACROSS = [(i, i ^ 1) for i in range(8)]
CAP = 6
OVER_LAST = (((1,), (1,)), ((), ()))
FIRST, SECOND = pl.ds(0, 768), pl.ds(768, 896)


def gelu_parts(value):
    normal_cdf = 0.5 * (1.0 + lax.erf(value * inv_root_two))
    slope = normal_cdf + value * jnp.exp(-0.5 * value * value) * inv_root_tau
    return (value * normal_cdf, slope)


def right(x):
    return lax.ppermute(x, "dp", RIGHT)


def left(x):
    return lax.ppermute(x, "dp", LEFT)


def across(x):
    return lax.ppermute(x, "dp", ACROSS)


def swapped(x, mask):
    return lax.ppermute(x, ("dp", "expert"), [(i, i ^ mask) for i in range(256)])


def add16(*terms):
    total = terms[0].astype(f32)
    for term in terms[1:]:
        total = total + term.astype(f32)
    return total.astype(bf16)


def chip_exchange(x):
    groups = [[2 * n + core for n in range(16)] for core in (0, 1)]
    x = x.reshape(16, x.shape[0] // 16, x.shape[1])
    x = lax.all_to_all(x, "expert", 0, 0, axis_index_groups=groups, tiled=True)
    return x.reshape(-1, x.shape[2])


def layer_norm(tokens):
    floats = tokens.astype(f32)
    centered = floats - jnp.mean(floats, axis=-1, keepdims=True)
    deviation = lax.rsqrt(jnp.mean(centered * centered, axis=-1, keepdims=True) + 1e-06)
    return centered * deviation, deviation


def dispatch_kernel(*refs):
    given, (gain, shift, near, far), (tok, idx, slot, comb, both, sems) = refs[:5], refs[5:9], refs[9:]
    places = (tok, both.at[pl.ds(128, 128)], idx, slot, comb)
    copies = [pltpu.make_async_copy(a, b, sems.at[n]) for n, (a, b) in enumerate(zip(given, places))]
    for copy in copies:
        copy.start()
    for copy in copies:
        copy.wait()
    standardized, _ = layer_norm(tok[...])
    both[:128, :] = (standardized * gain[...].reshape(1, -1) + shift[...].reshape(1, -1)).astype(bf16)
    expert = idx[...]
    core = (expert ^ lax.axis_index("expert")) & 1
    code = jnp.where(slot[...] >= 0, core * 192 + (expert >> 1) * 12 + slot[...], -1000)
    for part, out in enumerate((near, far)):
        row = lax.broadcasted_iota(jnp.int32, (192, 128), 0) + part * 192
        ins = [(code[k : k + 1, :] == row).astype(f32) for k in (0, 1)]
        outs = [(code[k : k + 1, :] + CAP == row).astype(f32) for k in (0, 1)]
        scale = jnp.sum(
            ins[0] + ins[1] + outs[0] * comb[0:1, :] + outs[1] * comb[1:2, :], axis=1, keepdims=True
        )
        table = jnp.concatenate([ins[0] + ins[1], outs[0] + outs[1]], axis=1).astype(bf16)
        picked = jnp.dot(table, both[...], preferred_element_type=f32)
        out[...] = (picked * scale).astype(bf16)


def regroup_kernel(count, table, *refs):
    ins, outs, buffer = refs[:count], refs[count:-1], refs[-1]
    size = ins[0].shape[0]
    for n, ref in enumerate(ins):
        buffer[n * size : (n + 1) * size, :] = ref[...]
    start = 0
    for out in outs:
        columns = out.shape[1]
        out[...] = jnp.dot(
            table[...], buffer[:, start : start + columns], preferred_element_type=f32
        ).astype(bf16)
        start += columns


def regroup(order, pieces, widths):
    rows, width = pieces[0].shape
    whole = rows * len(pieces)
    table = jnp.asarray(order[:, None] == np.arange(whole)[None, :], bf16)
    return pl.pallas_call(
        functools.partial(regroup_kernel, len(pieces)),
        out_shape=[jax.ShapeDtypeStruct((whole, n), bf16) for n in widths],
        scratch_shapes=[pltpu.VMEM((whole, width), bf16)],
        compiler_params=pltpu.CompilerParams(vmem_limit_bytes=24 * 2**20),
        cost_estimate=pl.CostEstimate(flops=1, bytes_accessed=1, transcendentals=0),
    )(table, *pieces)


def experts_kernel(blocks, parts, place, aliased, *refs):
    given, bias_in, refs = refs[:2], refs[2], refs[3:]
    whole_blocks = [refs[n * blocks : (n + 1) * blocks] for n in range(parts)]
    refs = refs[parts * blocks + 4 * aliased :]
    all_in, all_gr, all_act, all_pre, bias, sums = refs[:6]
    partials, scratch = refs[6:-8], refs[-8:]
    weight_in, weight_out, inputs, grads, act, grad_pre, sems, out_sems = scratch
    rows = 192 * blocks
    copies = []
    for b in range(blocks):
        r = pl.ds(192 * b, 192)
        for n, (kind, whole) in enumerate(((pl.ds(0, 192), inputs), (pl.ds(192, 192), grads))):
            first = whole_blocks[0][b].at[kind]
            second = whole_blocks[1][b].at[kind] if parts == 2 else whole_blocks[1 + n][b]
            for m, (part, columns) in enumerate(((first, FIRST), (second, SECOND))):
                sem = sems.at[4 * b + 2 * n + m]
                copies.append(pltpu.make_async_copy(part, whole.at[r, columns], sem))
    weights = [
        pltpu.make_async_copy(a, b, sems.at[4 * blocks + n])
        for n, (a, b) in enumerate(zip(given, (weight_in, weight_out)))
    ]
    weights[0].start()
    for copy in copies:
        copy.start()
    weights[1].start()
    weights[0].wait()
    for copy in copies:
        copy.wait()
    there = pl.ds(place, rows)
    keep = [
        pltpu.make_async_copy(here, out.at[there], out_sems.at[n])
        for n, (here, out) in enumerate(
            [(inputs, all_in), (grads, all_gr), (act, all_act), (grad_pre, all_pre)]
        )
    ]
    keep[0].start()
    keep[1].start()
    pre = jnp.dot(inputs[...], weight_in[...], preferred_element_type=f32) + bias_in[...]
    act_value, slope = gelu_parts(pre)
    act[...] = act_value.astype(bf16)
    keep[2].start()
    weights[1].wait()
    grad = slope * lax.dot_general(
        grads[...], weight_out[...], OVER_LAST, preferred_element_type=f32
    )
    bias[...] = jnp.sum(grad, axis=0, keepdims=True)
    grad_pre[...] = grad.astype(bf16)
    keep[3].start()
    partial = lax.dot_general(
        grad_pre[...], weight_in[...], OVER_LAST, preferred_element_type=f32
    )
    sums[0:1, :] = jnp.sum(partial * inputs[...].astype(f32), axis=0, keepdims=True)
    sums[1:2, :] = jnp.sum(partial, axis=0, keepdims=True)
    partial = partial.astype(bf16)
    start = 0
    for out in partials:
        out[...] = partial[start : start + out.shape[0], :]
        start += out.shape[0]
    for copy in keep:
        copy.wait()


def experts_step(weights, bias_in, place, blocks, kept, sizes):
    rows = 192 * len(blocks)
    parts = len(blocks[0])
    width = weights[0].shape[0]
    vmem, anywhere = pl.BlockSpec(memory_space=pltpu.VMEM), pl.BlockSpec(memory_space=pltpu.HBM)
    first = 3 + parts * len(blocks)
    out = pl.pallas_call(
        functools.partial(experts_kernel, len(blocks), parts, place, kept is not None),
        in_specs=[anywhere] * 2 + [vmem] + [anywhere] * (parts * len(blocks) + (4 if kept else 0)),
        out_specs=[anywhere] * 4 + [vmem] * (2 + len(sizes)),
        out_shape=[
            jax.ShapeDtypeStruct((1536, width), bf16),
            jax.ShapeDtypeStruct((1536, width), bf16),
            jax.ShapeDtypeStruct((1536, 512), bf16),
            jax.ShapeDtypeStruct((1536, 512), bf16),
            jax.ShapeDtypeStruct((1, 512), f32),
            jax.ShapeDtypeStruct((2, width), f32),
        ]
        + [jax.ShapeDtypeStruct((n, width), bf16) for n in sizes],
        scratch_shapes=[
            pltpu.VMEM((width, 512), bf16),
            pltpu.VMEM((512, width), bf16),
            pltpu.VMEM((rows, width), bf16),
            pltpu.VMEM((rows, width), bf16),
            pltpu.VMEM((rows, 512), bf16),
            pltpu.VMEM((rows, 512), bf16),
            pltpu.SemaphoreType.DMA((4 * len(blocks) + 3,)),
            pltpu.SemaphoreType.DMA((4,)),
        ],
        input_output_aliases={first + n: n for n in range(4)} if kept else {},
        compiler_params=pltpu.CompilerParams(vmem_limit_bytes=60 * 2**20),
        cost_estimate=pl.CostEstimate(flops=1, bytes_accessed=1, transcendentals=0),
    )(
        *weights,
        bias_in,
        *[block[n] for n in range(parts) for block in blocks],
        *(kept or ()),
    )
    return out[:4], out[4], out[5], out[6:]


def return_kernel(table, summed, sums, out, buffer):
    buffer[:192, :] = summed[...]
    high = sums[...].astype(bf16).astype(f32)
    low = sums[...] - high
    row = lax.broadcasted_iota(jnp.int32, (16, sums.shape[1]), 0)
    rows = jnp.where(row == 0, high[0:1, :], jnp.where(row == 1, low[0:1, :], 0.0))
    rows = jnp.where(row == 2, high[1:2, :], jnp.where(row == 3, low[1:2, :], rows))
    buffer[192:, :] = rows.astype(bf16)
    out[...] = jnp.dot(table[...], buffer[...], preferred_element_type=f32).astype(bf16)


def return_rows(summed, sums):
    order = np.zeros((16, 16), np.int32)
    order[:, :12] = np.arange(192).reshape(16, 12)
    order[:, 12:] = 192 + np.arange(4)
    table = jnp.asarray(order.reshape(-1, 1) == np.arange(208)[None, :], bf16)
    width = summed.shape[1]
    return pl.pallas_call(
        return_kernel,
        out_shape=jax.ShapeDtypeStruct((256, width), bf16),
        scratch_shapes=[pltpu.VMEM((208, width), bf16)],
        compiler_params=pltpu.CompilerParams(vmem_limit_bytes=24 * 2**20),
    )(table, summed, sums)


def combine_kernel(tok, cot, idx, slot, gain, shift, near, far, out, gain_out, shift_out):
    def summed(ref):
        column = lax.broadcasted_iota(jnp.int32, (8, 256), 1) & 15
        row = lax.broadcasted_iota(jnp.int32, (8, 256), 0)
        table = (column >= 12) & (((column - 12) >> 1) == row)
        return jnp.dot(table.astype(f32).astype(bf16), ref[...], preferred_element_type=f32)

    sums = summed(near) + summed(far)
    gains = gain[...].reshape(1, -1)
    shift_out[...] = sums[1:2, :].reshape(-1)
    gain_out[...] = ((sums[0:1, :] - shift[...].reshape(1, -1) * sums[1:2, :]) / gains).reshape(-1)
    expert = idx[...]
    core = (expert ^ lax.axis_index("expert")) & 1
    code = jnp.where(slot[...] >= 0, core * 256 + (expert >> 1) * 16 + core * CAP + slot[...], -1000)
    normed_grad = jnp.zeros(tok.shape, f32)
    for part, ref in enumerate((near, far)):
        row = lax.broadcasted_iota(jnp.int32, (256, 128), 0) + part * 256
        table = (code[0:1, :] == row).astype(f32) + (code[1:2, :] == row).astype(f32)
        normed_grad = normed_grad + lax.dot_general(
            table.astype(bf16), ref[...], (((0,), (0,)), ((), ())), preferred_element_type=f32
        )
    standardized, deviation = layer_norm(tok[...])
    scaled = normed_grad * gains
    inner = (
        scaled
        - jnp.mean(scaled, axis=-1, keepdims=True)
        - standardized * jnp.mean(scaled * standardized, axis=-1, keepdims=True)
    )
    out[...] = (cot[...].astype(f32) + deviation * inner).astype(bf16)


def send_order():
    return np.arange(384).reshape(2, 16, 2, CAP).transpose(1, 2, 0, 3).reshape(-1)


def take_order():
    return np.arange(384).reshape(16, 2, 2 * CAP).transpose(1, 0, 2).reshape(-1)


def shards(tokens, cotangent, expert_idx, expert_slot, combine, gain, shift, w_in, b_in, w_out):
    width = tokens.shape[1]
    weight_in, weight_out = w_in[0], w_out[0]
    idx, slot, comb = expert_idx.T, expert_slot.T, combine.T
    gain_row, shift_row = gain, shift
    limit = pltpu.CompilerParams(vmem_limit_bytes=24 * 2**20)
    near, far = pl.pallas_call(
        dispatch_kernel,
        in_specs=[pl.BlockSpec(memory_space=pltpu.HBM)] * 5 + [pl.BlockSpec(memory_space=pltpu.VMEM)] * 2,
        out_shape=[jax.ShapeDtypeStruct((192, width), bf16)] * 2,
        scratch_shapes=[
            pltpu.VMEM((128, width), bf16),
            pltpu.VMEM((2, 128), jnp.int32),
            pltpu.VMEM((2, 128), jnp.int32),
            pltpu.VMEM((2, 128), f32),
            pltpu.VMEM((256, width), bf16),
            pltpu.SemaphoreType.DMA((5,)),
        ],
        compiler_params=pltpu.CompilerParams(vmem_limit_bytes=60 * 2**20),
    )(tokens, cotangent, idx, slot, comb, gain_row, shift_row)
    (packed,) = regroup(send_order(), [near, swapped(far, 1)], [width])
    own_a, own_b = regroup(take_order(), [chip_exchange(packed)], [768, 896])

    l_a, r_a, q_a = right(own_a), left(own_a), across(own_a)
    l_b, r_b, q_b = right(own_b), left(own_b), across(own_b)
    ql_a, f_a, qr_a = right(q_a), left(r_a), across(r_a)
    ql_b, f_b, qr_b = right(q_b), left(r_b), across(r_b)
    qf_a, qf_b = right(ql_a), left(qr_b)

    step = functools.partial(experts_step, (weight_in, weight_out), b_in)
    early = ((own_a, own_b), (l_a, l_b), (r_a, r_b), (q_a, q_b))
    early, _ = lax.optimization_barrier((early, ql_a))
    kept, bias_a, sums_a, (p_own, p_l, p_r, p_q) = step(0, early, None, [192] * 4)
    kept, bias_b, sums_b, (ql_low, ql_high, p_f, qr_low, qr_high) = step(
        768, ((ql_a, ql_b), (f_a, f_b), (qr_a, qr_b)), kept, [96, 96, 192, 96, 96]
    )
    kept, bias_c, sums_c, (low, high) = step(1344, ((qf_a, qf_b),), kept, [96] * 2)
    back_ql, back_qr = left(low), right(high)
    sums = sums_a + sums_b + sums_c
    across_sums = swapped(sums, 32)
    back_qr, across_sums = lax.optimization_barrier((back_qr, across_sums))
    sums = sums + across_sums
    sums = (sums + swapped(sums, 128)) + (swapped(sums, 64) + swapped(sums, 192))
    cat = lambda *a: jnp.concatenate(a, axis=0)
    s_ql = cat(add16(ql_low, back_ql), ql_high)
    s_qr = cat(qr_low, add16(qr_high, back_qr))
    p_f, _ = lax.optimization_barrier((p_f, back_qr))
    back_q, back_f, back_r = left(s_ql), right(p_f), across(s_qr)
    s_q = add16(p_q, back_q)
    s_r = add16(p_r, back_f, back_r)
    p_l, _, _ = lax.optimization_barrier((p_l, s_q, s_r))
    summed = add16(p_own, left(p_l), right(s_r), across(s_q))

    over_rows = (((0,), (0,)), ((), ()))
    dot = functools.partial(lax.dot_general, dimension_numbers=over_rows, preferred_element_type=f32)
    inputs, grads, act, grad_pre = kept
    grad_win = dot(inputs, grad_pre)
    grad_wout = dot(act, grads)
    grad_bias = bias_a + bias_b + bias_c
    summed, grad_win = lax.optimization_barrier((summed, grad_win))
    came = chip_exchange(return_rows(summed, sums))
    came, grad_wout = lax.optimization_barrier((came, grad_wout))
    grad_tokens, gain_gradient, grad_shift = pl.pallas_call(
        combine_kernel,
        out_shape=[jax.ShapeDtypeStruct(tokens.shape, bf16)] + [jax.ShapeDtypeStruct((width,), f32)] * 2,
        compiler_params=limit,
    )(tokens, cotangent, idx, slot, gain_row, shift_row, came, swapped(came, 1))
    return (
        grad_tokens,
        grad_win[None],
        grad_bias,
        grad_wout[None],
        gain_gradient,
        grad_shift,
    )


def solution(mesh):
    both = P(("dp", "expert"), None)
    return jax.shard_map(
        shards,
        mesh=mesh,
        in_specs=(both,) * 5
        + (P(), P(), P("expert", None, "dp"), P("expert", "dp"), P("expert", "dp", None)),
        out_specs=(both, P("expert", None, "dp"), P("expert", "dp"), P("expert", "dp", None), P(), P()),
        check_vma=False,
    )
```

profile of v0, /device:TPU:1, one launch (start us, length us, event | category | flops | bytes accessed | tf_op | source)
XLA Modules:
  0.0 220.3 jit_solution(11203689568680127634)
XLA Ops:
  0.6 3.6 %shard_map.172 = (bf16[192,1664]{1,0:T(8,128)(2,1)}, bf16[192,1664]{1,0:T(8,128)(2,1)}) custom-call(bf16[128,1664]{1,0:T(8,128)(2,1)} %tok.1, bf16[128,1664]{1,0:T(8,128)(2,1)} %cot.1, s32[2,128]{1,0:T(2,128)} %bitcast.19, s32[2,128]{1,0:T(2,128)} %bitcast.21, f32[2,128]{1,0:T(2,128)} %bitcast.29, f32[1664]{0:T(1024)} %gain.1, f32[1664]{0:T(1024)} %shift.1), custom_call_target="tpu_custom_call" | custom-call | tf_op jit(solution)/shard_map/pallas_call | solution.py:292
  4.2 3.3 %collective-permute-start = (bf16[192,1664]{1,0:T(8,128)(2,1)}, bf16[192,1664]{1,0:T(8,128)(2,1)S(1)}, u32[]{:S(2)}, u32[]{:S(2)}) collective-permute-start(bf16[192,1664]{1,0:T(8,128)(2,1)} %get-tuple-element.59), channel_id=1, source_target_pairs={{0,1},{1,0},{2,3},{3,2},{4,5},{5,4},{6,7},{7,6},{8,9},{9,8},{10,11... | collective-permute-start | bytes 1916936 | tf_op jit(solution)/shard_map/ppermute | solution.py:43
  7.6 1.9 collective-permute-done.refs_1_
  12.4 42.3 %all_to_all.10 = bf16[16,24,1664]{2,1,0:T(8,128)(2,1)S(1)} all-to-all(bf16[16,24,1664]{2,1,0:T(8,128)(2,1)S(1)} %bitcast.16), channel_id=1, replica_groups={{0,2,4,6,8,10,12,14,16,18,20,22,24,26,28,30},{1,3,5,7,9,11,13,15,17,19,..., dimensions={0} | all-to-all | bytes 2555904 | tf_op jit(solution)/shard_map/all_to_all | solution.py:56
  55.6 2.6 %collective-permute-start.4 = (bf16[384,896]{1,0:T(8,128)(2,1)S(1)}, bf16[384,896]{1,0:T(8,128)(2,1)S(1)}, u32[]{:S(2)}, u32[]{:S(2)}) collective-permute-start(bf16[384,896]{1,0:T(8,128)(2,1)S(1)} %get-tuple-element.66.refs_7_), channel_id=1, source_target_pairs={{0,192},{32,224},{64,0},{96,32},{128,64},{160,96},{192,128},{224,1... | collective-permute-start | bytes 2064392 | tf_op jit(solution)/shard_map/ppermute | solution.py:35
  61.0 8.6 %collective-permute-done.5.refs_6_ = bf16[384,768]{1,0:T(8,128)(2,1)S(1)} collective-permute-done((bf16[384,768]{1,0:T(8,128)(2,1)S(1)}, bf16[384,768]{1,0:T(8,128)(2,1)S(1)}, u32[]{:S(2)}, u32[]{:S(2)}) %collective-permute-start.5) | collective-permute-done | bytes 589856 | tf_op jit(solution)/shard_map/ppermute | solution.py:39
  70.9 11.6 %collective-permute-done.3.refs_5_ = bf16[384,768]{1,0:T(8,128)(2,1)} collective-permute-done((bf16[384,768]{1,0:T(8,128)(2,1)S(1)}, bf16[384,768]{1,0:T(8,128)(2,1)}, u32[]{:S(2)}, u32[]{:S(2)}) %collective-permute-start.3) | collective-permute-done | bytes 589856 | tf_op jit(solution)/shard_map/ppermute | solution.py:35
  83.0 3.1 %collective-permute-start.8 = (bf16[384,768]{1,0:T(8,128)(2,1)}, bf16[384,768]{1,0:T(8,128)(2,1)}, u32[]{:S(2)}, u32[]{:S(2)}) collective-permute-start(bf16[384,768]{1,0:T(8,128)(2,1)} %collective-permute-done.3.refs_5_), channel_id=1, source_target_pairs={{0,192},{32,224},{64,0},{96,32},{128,64},{160,96},{192,128},{224,1... | collective-permute-start | bytes 1769480 | tf_op jit(solution)/shard_map/ppermute | solution.py:35
  86.1 1.4 collective-permute-start.11
  87.5 11.7 %collective-permute-done.12.refs_8_ = bf16[384,896]{1,0:T(8,128)(2,1)} collective-permute-done((bf16[384,896]{1,0:T(8,128)(2,1)S(1)}, bf16[384,896]{1,0:T(8,128)(2,1)}, u32[]{:S(2)}, u32[]{:S(2)}) %collective-permute-start.12) | collective-permute-done | bytes 688160 | tf_op jit(solution)/shard_map/ppermute | solution.py:39
  100.0 1.3 collective-permute-start.9
  102.0 10.5 %shard_map.175 = (bf16[1536,1664]{1,0:T(8,128)(2,1)}, bf16[1536,1664]{1,0:T(8,128)(2,1)}, bf16[1536,512]{1,0:T(8,128)(2,1)}, bf16[1536,512]{1,0:T(8,128)(2,1)}, ...) custom-call(bf16[1664,512]{1,0:T(8,128)(2,1)} %bitcast.23, ...), custom_call_target="tpu_custom_call" | custom-call | flops 1 | bytes 1 | tf_op jit(solution)/shard_map/pallas_call | solution.py:187
  112.6 2.2 collective-permute-done.10.refs_6_
  114.8 8.7 %shard_map.176 = (bf16[1536,1664]{1,0:T(8,128)(2,1)}, bf16[1536,1664]{1,0:T(8,128)(2,1)}, bf16[1536,512]{1,0:T(8,128)(2,1)}, bf16[1536,512]{1,0:T(8,128)(2,1)}, ...) custom-call(bf16[1664,512]{1,0:T(8,128)(2,1)} %bitcast.24, ...), custom_call_target="tpu_custom_call", output_to_operand_aliasing={{0}: (9, {}), {1}: (10, {}), {2}: (11, {}), {3}: (12, {})} | custom-call | flops 1 | bytes 1 | tf_op jit(solution)/shard_map/pallas_call | solution.py:187
  123.4 4.0 %collective-permute-done.13.refs_3_ = bf16[384,768]{1,0:T(8,128)(2,1)} collective-permute-done((bf16[384,768]{1,0:T(8,128)(2,1)}, bf16[384,768]{1,0:T(8,128)(2,1)}, u32[]{:S(2)}, u32[]{:S(2)}) %collective-permute-start.13) | collective-permute-done | bytes 589856 | tf_op jit(solution)/shard_map/ppermute | solution.py:31
  128.3 5.6 %shard_map.177 = (bf16[1536,1664]{1,0:T(8,128)(2,1)}, bf16[1536,1664]{1,0:T(8,128)(2,1)}, bf16[1536,512]{1,0:T(8,128)(2,1)}, bf16[1536,512]{1,0:T(8,128)(2,1)}, ...) custom-call(bf16[1664,512]{1,0:T(8,128)(2,1)} %bitcast.25, ...), custom_call_target="tpu_custom_call", output_to_operand_aliasing={{0}: (5, {}), {1}: (6, {}), {2}: (7, {}), {3}: (8, {})} | custom-call | flops 1 | bytes 1 | tf_op jit(solution)/shard_map/pallas_call | solution.py:187
  135.9 2.6 %collective-permute-start.15 = (bf16[96,1664]{1,0:T(8,128)(2,1)}, bf16[96,1664]{1,0:T(8,128)(2,1)S(1)}, u32[]{:S(2)}, u32[]{:S(2)}) collective-permute-start(bf16[96,1664]{1,0:T(8,128)(2,1)} %get-tuple-element.82), channel_id=1, source_target_pairs={{0,192},{32,224},{64,0},{96,32},{128,64},{160,96},{192,128},{224,1... | collective-permute-start | bytes 958472 | tf_op jit(solution)/shard_map/ppermute | solution.py:35
  138.5 2.7 %collective-permute-done.17 = bf16[96,1664]{1,0:T(8,128)(2,1)S(1)} collective-permute-done((bf16[96,1664]{1,0:T(8,128)(2,1)}, bf16[96,1664]{1,0:T(8,128)(2,1)S(1)}, u32[]{:S(2)}, u32[]{:S(2)}) %collective-permute-start.17) | collective-permute-done | bytes 319520 | tf_op jit(solution)/shard_map/ppermute | solution.py:31
  141.2 9.4 %collective-permute-start.19 = (bf16[192,1664]{1,0:T(8,128)(2,1)S(1)}, bf16[192,1664]{1,0:T(8,128)(2,1)S(1)}, u32[]{:S(2)}, u32[]{:S(2)}) collective-permute-start(bf16[192,1664]{1,0:T(8,128)(2,1)S(1)} %copy-done.34), channel_id=1, source_target_pairs={{0,64},{32,96},{64,128},{96,160},{128,192},{160,224},{192,0},{224,... | collective-permute-start | bytes 1916936 | tf_op jit(solution)/shard_map/ppermute | solution.py:31
  152.1 2.7 %collective-permute-start.16 = (bf16[192,1664]{1,0:T(8,128)(2,1)S(1)}, bf16[192,1664]{1,0:T(8,128)(2,1)S(1)}, u32[]{:S(2)}, u32[]{:S(2)}) collective-permute-start(bf16[192,1664]{1,0:T(8,128)(2,1)S(1)} %pad_maximum_fusion), channel_id=1, source_target_pairs={{0,192},{32,224},{64,0},{96,32},{128,64},{160,96},{192,128},{224,1... | collective-permute-start | bytes 1916936 | tf_op jit(solution)/shard_map/ppermute | solution.py:35
  155.5 7.6 %collective-permute-done.19 = bf16[192,1664]{1,0:T(8,128)(2,1)S(1)} collective-permute-done((bf16[192,1664]{1,0:T(8,128)(2,1)S(1)}, bf16[192,1664]{1,0:T(8,128)(2,1)S(1)}, u32[]{:S(2)}, u32[]{:S(2)}) %collective-permute-start.19) | collective-permute-done | bytes 639008 | tf_op jit(solution)/shard_map/ppermute | solution.py:31
  163.6 1.4 collective-permute-start.23
  165.0 2.8 %collective-permute-start.21 = (bf16[192,1664]{1,0:T(8,128)(2,1)S(1)}, bf16[192,1664]{1,0:T(8,128)(2,1)S(1)}, u32[]{:S(2)}, u32[]{:S(2)}) collective-permute-start(bf16[192,1664]{1,0:T(8,128)(2,1)S(1)} %copy-done.33), channel_id=1, source_target_pairs={{0,192},{32,224},{64,0},{96,32},{128,64},{160,96},{192,128},{224,1... | collective-permute-start | bytes 1916936 | tf_op jit(solution)/shard_map/ppermute | solution.py:35
  167.8 4.6 %fusion = f32[1664,512]{1,0:T(8,128)} fusion(bf16[1536,1664]{1,0:T(8,128)(2,1)S(1)} %copy-done.12, bf16[1536,512]{1,0:T(8,128)(2,1)S(1)} %copy-done.14), kind=kOutput, calls=%fused_computation.10 | convolution fusion | flops 2617245696 | bytes 10092544 | tf_op jit(solution)/shard_map/dot_general | solution.py:342
  172.5 4.4 %collective-permute-done.21 = bf16[192,1664]{1,0:T(8,128)(2,1)S(1)} collective-permute-done((bf16[192,1664]{1,0:T(8,128)(2,1)S(1)}, bf16[192,1664]{1,0:T(8,128)(2,1)S(1)}, u32[]{:S(2)}, u32[]{:S(2)}) %collective-permute-start.21) | collective-permute-done | bytes 639008 | tf_op jit(solution)/shard_map/ppermute | solution.py:35
  177.8 1.4 shard_map.178
  179.2 10.1 %all-to-all-start.1 = ((bf16[16,16,1664]{2,1,0:T(8,128)(2,1)}), bf16[16,16,1664]{2,1,0:T(8,128)(2,1)S(1)}, u32[]{:S(2)}, u32[]{:S(2)}) async-start(bf16[16,16,1664]{2,1,0:T(8,128)(2,1)} %bitcast.7), calls=%async_computation.1 | async-start | bytes 1703936 | tf_op jit(solution)/shard_map/all_to_all | solution.py:56
  189.4 7.3 %fusion.1 = f32[512,1664]{1,0:T(8,128)} fusion(bf16[1536,512]{1,0:T(8,128)(2,1)S(1)} %copy-done.13, bf16[1536,1664]{1,0:T(8,128)(2,1)} %get-tuple-element.100), kind=kOutput, calls=%fused_computation.11 | convolution fusion | flops 2617245696 | bytes 10092544 | tf_op jit(solution)/shard_map/dot_general | solution.py:343
  196.7 10.1 %all-to-all-done.1 = bf16[16,16,1664]{2,1,0:T(8,128)(2,1)S(1)} async-done(((bf16[16,16,1664]{2,1,0:T(8,128)(2,1)}), bf16[16,16,1664]{2,1,0:T(8,128)(2,1)S(1)}, u32[]{:S(2)}, u32[]{:S(2)}) %all-to-all-start.1) | async-done | bytes 852000 | tf_op jit(solution)/shard_map/all_to_all | solution.py:56
  206.8 9.5 %collective-permute-start.27 = (bf16[256,1664]{1,0:T(8,128)(2,1)S(1)}, bf16[256,1664]{1,0:T(8,128)(2,1)S(1)}, u32[]{:S(2)}, u32[]{:S(2)}) collective-permute-start(bf16[256,1664]{1,0:T(8,128)(2,1)S(1)} %bitcast.17), channel_id=1, source_target_pairs={{0,1},{1,0},{2,3},{3,2},{4,5},{5,4},{6,7},{7,6},{8,9},{9,8},{10,11... | collective-permute-start | bytes 2555912 | tf_op jit(solution)/shard_map/ppermute | solution.py:43
  217.0 1.4 collective-permute-done.27.far
  218.4 1.7 shard_map.179
  (118 shorter events, 17.1 us)
Async XLA Ops:
  4.2 5.2 %collective-permute-start = (bf16[192,1664]{1,0:T(8,128)(2,1)}, bf16[192,1664]{1,0:T(8,128)(2,1)S(1)}, u32[]{:S(2)}, u32[]{:S(2)}) collective-permute-start(bf16[192,1664]{1,0:T(8,128)(2,1)} %get-tuple-element.59), channel_id=1, source_target_pairs={{0,1},{1,0},{2,3},{3,2},{4,5},{5,4},{6,7},{7,6},{8,9},{9,8},{10,11... | collective-permute-start | bytes 1916936 | tf_op jit(solution)/shard_map/ppermute | solution.py:43
  12.4 42.3 %copy-start.6 = (bf16[384,384]{1,0:T(8,128)(2,1)S(1)}, bf16[384,384]{1,0:T(8,128)(2,1)}, u32[]{:S(2)}) copy-start(bf16[384,384]{1,0:T(8,128)(2,1)} %constant.7.clone.table) | copy-start | bytes 884740
  55.5 46.5 %copy-start.2 = (bf16[384,896]{1,0:T(8,128)(2,1)}, bf16[384,896]{1,0:T(8,128)(2,1)S(1)}, u32[]{:S(2)}) copy-start(bf16[384,896]{1,0:T(8,128)(2,1)S(1)} %get-tuple-element.66.refs_7_) | copy-start | bytes 2064388
  55.5 46.5 %copy-start.4 = (bf16[384,768]{1,0:T(8,128)(2,1)}, bf16[384,768]{1,0:T(8,128)(2,1)S(1)}, u32[]{:S(2)}) copy-start(bf16[384,768]{1,0:T(8,128)(2,1)S(1)} %get-tuple-element.62.refs_3_) | copy-start | bytes 1769476
  55.6 14.2 %collective-permute-start.4 = (bf16[384,896]{1,0:T(8,128)(2,1)S(1)}, bf16[384,896]{1,0:T(8,128)(2,1)S(1)}, u32[]{:S(2)}, u32[]{:S(2)}) collective-permute-start(bf16[384,896]{1,0:T(8,128)(2,1)S(1)} %get-tuple-element.66.refs_7_), channel_id=1, source_target_pairs={{0,192},{32,224},{64,0},{96,32},{128,64},{160,96},{192,128},{224,1... | collective-permute-start | bytes 2064392 | tf_op jit(solution)/shard_map/ppermute | solution.py:35
  58.1 11.5 %collective-permute-start.5 = (bf16[384,768]{1,0:T(8,128)(2,1)S(1)}, bf16[384,768]{1,0:T(8,128)(2,1)S(1)}, u32[]{:S(2)}, u32[]{:S(2)}) collective-permute-start(bf16[384,768]{1,0:T(8,128)(2,1)S(1)} %get-tuple-element.62.refs_3_), channel_id=1, source_target_pairs={{0,32},{32,0},{64,96},{96,64},{128,160},{160,128},{192,224},{224,1... | collective-permute-start | bytes 1769480 | tf_op jit(solution)/shard_map/ppermute | solution.py:39
  58.6 23.9 %collective-permute-start.3 = (bf16[384,768]{1,0:T(8,128)(2,1)S(1)}, bf16[384,768]{1,0:T(8,128)(2,1)}, u32[]{:S(2)}, u32[]{:S(2)}) collective-permute-start(bf16[384,768]{1,0:T(8,128)(2,1)S(1)} %get-tuple-element.62.refs_3_), channel_id=1, source_target_pairs={{0,192},{32,224},{64,0},{96,32},{128,64},{160,96},{192,128},{224,1... | collective-permute-start | bytes 1769480 | tf_op jit(solution)/shard_map/ppermute | solution.py:35
  59.1 23.9 %collective-permute-start.1 = (bf16[384,768]{1,0:T(8,128)(2,1)S(1)}, bf16[384,768]{1,0:T(8,128)(2,1)S(1)}, u32[]{:S(2)}, u32[]{:S(2)}) collective-permute-start(bf16[384,768]{1,0:T(8,128)(2,1)S(1)} %get-tuple-element.62.refs_3_), channel_id=1, source_target_pairs={{0,64},{32,96},{64,128},{96,160},{128,192},{160,224},{192,0},{224,... | collective-permute-start | bytes 1769480 | tf_op jit(solution)/shard_map/ppermute | solution.py:31
  60.0 26.0 %collective-permute-start.6 = (bf16[384,896]{1,0:T(8,128)(2,1)S(1)}, bf16[384,896]{1,0:T(8,128)(2,1)S(1)}, u32[]{:S(2)}, u32[]{:S(2)}) collective-permute-start(bf16[384,896]{1,0:T(8,128)(2,1)S(1)} %get-tuple-element.66.refs_7_), channel_id=1, source_target_pairs={{0,32},{32,0},{64,96},{96,64},{128,160},{160,128},{192,224},{224,1... | collective-permute-start | bytes 2064392 | tf_op jit(solution)/shard_map/ppermute | solution.py:39
  69.6 17.8 %collective-permute-start.2 = (bf16[384,896]{1,0:T(8,128)(2,1)S(1)}, bf16[384,896]{1,0:T(8,128)(2,1)S(1)}, u32[]{:S(2)}, u32[]{:S(2)}) collective-permute-start(bf16[384,896]{1,0:T(8,128)(2,1)S(1)} %get-tuple-element.66.refs_7_), channel_id=1, source_target_pairs={{0,64},{32,96},{64,128},{96,160},{128,192},{160,224},{192,0},{224,... | collective-permute-start | bytes 2064392 | tf_op jit(solution)/shard_map/ppermute | solution.py:31
  69.8 29.4 %collective-permute-start.12 = (bf16[384,896]{1,0:T(8,128)(2,1)S(1)}, bf16[384,896]{1,0:T(8,128)(2,1)}, u32[]{:S(2)}, u32[]{:S(2)}) collective-permute-start(bf16[384,896]{1,0:T(8,128)(2,1)S(1)} %collective-permute-done.4.refs_9_), channel_id=1, source_target_pairs={{0,32},{32,0},{64,96},{96,64},{128,160},{160,128},{192,224},{224,1... | collective-permute-start | bytes 2064392 | tf_op jit(solution)/shard_map/ppermute | solution.py:39
  82.4 17.6 %collective-permute-start.7 = (bf16[384,768]{1,0:T(8,128)(2,1)S(1)}, bf16[384,768]{1,0:T(8,128)(2,1)}, u32[]{:S(2)}, u32[]{:S(2)}) collective-permute-start(bf16[384,768]{1,0:T(8,128)(2,1)S(1)} %collective-permute-done.5.refs_6_), channel_id=1, source_target_pairs={{0,64},{32,96},{64,128},{96,160},{128,192},{160,224},{192,0},{224,... | collective-permute-start | bytes 1769480 | tf_op jit(solution)/shard_map/ppermute | solution.py:31
  83.0 18.3 %collective-permute-start.8 = (bf16[384,768]{1,0:T(8,128)(2,1)}, bf16[384,768]{1,0:T(8,128)(2,1)}, u32[]{:S(2)}, u32[]{:S(2)}) collective-permute-start(bf16[384,768]{1,0:T(8,128)(2,1)} %collective-permute-done.3.refs_5_), channel_id=1, source_target_pairs={{0,192},{32,224},{64,0},{96,32},{128,64},{160,96},{192,128},{224,1... | collective-permute-start | bytes 1769480 | tf_op jit(solution)/shard_map/ppermute | solution.py:35
  86.1 26.5 %collective-permute-start.11 = (bf16[384,896]{1,0:T(8,128)(2,1)S(1)}, bf16[384,896]{1,0:T(8,128)(2,1)}, u32[]{:S(2)}, u32[]{:S(2)}) collective-permute-start(bf16[384,896]{1,0:T(8,128)(2,1)S(1)} %collective-permute-done.4.refs_9_), channel_id=1, source_target_pairs={{0,192},{32,224},{64,0},{96,32},{128,64},{160,96},{192,128},{224,1... | collective-permute-start | bytes 2064392 | tf_op jit(solution)/shard_map/ppermute | solution.py:35
  87.4 27.3 %collective-permute-start.10 = (bf16[384,896]{1,0:T(8,128)(2,1)S(1)}, bf16[384,896]{1,0:T(8,128)(2,1)}, u32[]{:S(2)}, u32[]{:S(2)}) collective-permute-start(bf16[384,896]{1,0:T(8,128)(2,1)S(1)} %collective-permute-done.6.refs_10_), channel_id=1, source_target_pairs={{0,64},{32,96},{64,128},{96,160},{128,192},{160,224},{192,0},{224,... | collective-permute-start | bytes 2064392 | tf_op jit(solution)/shard_map/ppermute | solution.py:31
  99.2 28.2 %collective-permute-start.14 = (bf16[384,896]{1,0:T(8,128)(2,1)}, bf16[384,896]{1,0:T(8,128)(2,1)S(1)}, u32[]{:S(2)}, u32[]{:S(2)}) collective-permute-start(bf16[384,896]{1,0:T(8,128)(2,1)} %collective-permute-done.12.refs_8_), channel_id=1, source_target_pairs={{0,192},{32,224},{64,0},{96,32},{128,64},{160,96},{192,128},{224,1... | collective-permute-start | bytes 2064392 | tf_op jit(solution)/shard_map/ppermute | solution.py:35
  100.0 12.6 %collective-permute-start.9 = (bf16[384,768]{1,0:T(8,128)(2,1)}, bf16[384,768]{1,0:T(8,128)(2,1)}, u32[]{:S(2)}, u32[]{:S(2)}) collective-permute-start(bf16[384,768]{1,0:T(8,128)(2,1)} %collective-permute-done.3.refs_5_), channel_id=1, source_target_pairs={{0,32},{32,0},{64,96},{96,64},{128,160},{160,128},{192,224},{224,1... | collective-permute-start | bytes 1769480 | tf_op jit(solution)/shard_map/ppermute | solution.py:39
  101.3 26.1 %collective-permute-start.13 = (bf16[384,768]{1,0:T(8,128)(2,1)}, bf16[384,768]{1,0:T(8,128)(2,1)}, u32[]{:S(2)}, u32[]{:S(2)}) collective-permute-start(bf16[384,768]{1,0:T(8,128)(2,1)} %collective-permute-done.7.refs_3_), channel_id=1, source_target_pairs={{0,64},{32,96},{64,128},{96,160},{128,192},{160,224},{192,0},{224,... | collective-permute-start | bytes 1769480 | tf_op jit(solution)/shard_map/ppermute | solution.py:31
  133.9 7.3 %collective-permute-start.17 = (bf16[96,1664]{1,0:T(8,128)(2,1)}, bf16[96,1664]{1,0:T(8,128)(2,1)S(1)}, u32[]{:S(2)}, u32[]{:S(2)}) collective-permute-start(bf16[96,1664]{1,0:T(8,128)(2,1)} %get-tuple-element.86), channel_id=1, source_target_pairs={{0,64},{32,96},{64,128},{96,160},{128,192},{160,224},{192,0},{224,... | collective-permute-start | bytes 958472 | tf_op jit(solution)/shard_map/ppermute | solution.py:31
  134.7 3.8 %collective-permute-start.18 = (f32[2,1664]{1,0:T(2,128)S(1)}, f32[2,1664]{1,0:T(2,128)S(1)}, u32[]{:S(2)}, u32[]{:S(2)}) collective-permute-start(f32[2,1664]{1,0:T(2,128)S(1)} %add_add_fusion.1), channel_id=1, source_target_pairs={{0,32},{1,33},{2,34},{3,35},{4,36},{5,37},{6,38},{7,39},{8,40},{9,... | collective-permute-start | bytes 39944 | tf_op jit(solution)/shard_map/ppermute | solution.py:43
  135.9 16.1 %collective-permute-start.15 = (bf16[96,1664]{1,0:T(8,128)(2,1)}, bf16[96,1664]{1,0:T(8,128)(2,1)S(1)}, u32[]{:S(2)}, u32[]{:S(2)}) collective-permute-start(bf16[96,1664]{1,0:T(8,128)(2,1)} %get-tuple-element.82), channel_id=1, source_target_pairs={{0,192},{32,224},{64,0},{96,32},{128,64},{160,96},{192,128},{224,1... | collective-permute-start | bytes 958472 | tf_op jit(solution)/shard_map/ppermute | solution.py:35
  141.2 21.9 %collective-permute-start.19 = (bf16[192,1664]{1,0:T(8,128)(2,1)S(1)}, bf16[192,1664]{1,0:T(8,128)(2,1)S(1)}, u32[]{:S(2)}, u32[]{:S(2)}) collective-permute-start(bf16[192,1664]{1,0:T(8,128)(2,1)S(1)} %copy-done.34), channel_id=1, source_target_pairs={{0,64},{32,96},{64,128},{96,160},{128,192},{160,224},{192,0},{224,... | collective-permute-start | bytes 1916936 | tf_op jit(solution)/shard_map/ppermute | solution.py:31
  150.8 12.3 %collective-permute-start.20 = (bf16[192,1664]{1,0:T(8,128)(2,1)S(1)}, bf16[192,1664]{1,0:T(8,128)(2,1)S(1)}, u32[]{:S(2)}, u32[]{:S(2)}) collective-permute-start(bf16[192,1664]{1,0:T(8,128)(2,1)S(1)} %pad_maximum_fusion.1), channel_id=1, source_target_pairs={{0,32},{32,0},{64,96},{96,64},{128,160},{160,128},{192,224},{224,1... | collective-permute-start | bytes 1916936 | tf_op jit(solution)/shard_map/ppermute | solution.py:39
  152.1 11.4 %collective-permute-start.16 = (bf16[192,1664]{1,0:T(8,128)(2,1)S(1)}, bf16[192,1664]{1,0:T(8,128)(2,1)S(1)}, u32[]{:S(2)}, u32[]{:S(2)}) collective-permute-start(bf16[192,1664]{1,0:T(8,128)(2,1)S(1)} %pad_maximum_fusion), channel_id=1, source_target_pairs={{0,192},{32,224},{64,0},{96,32},{128,64},{160,96},{192,128},{224,1... | collective-permute-start | bytes 1916936 | tf_op jit(solution)/shard_map/ppermute | solution.py:35
  154.8 10.2 %collective-permute-start.24 = (f32[2,1664]{1,0:T(2,128)S(1)}, f32[2,1664]{1,0:T(2,128)S(1)}, u32[]{:S(2)}, u32[]{:S(2)}) collective-permute-start(f32[2,1664]{1,0:T(2,128)S(1)} %add.58), channel_id=1, source_target_pairs={{0,128},{1,129},{2,130},{3,131},{4,132},{5,133},{6,134},{7,135},{8... | collective-permute-start | bytes 39944 | tf_op jit(solution)/shard_map/ppermute | solution.py:43
  154.9 17.5 %collective-permute-start.25 = (f32[2,1664]{1,0:T(2,128)S(1)}, f32[2,1664]{1,0:T(2,128)S(1)}, u32[]{:S(2)}, u32[]{:S(2)}) collective-permute-start(f32[2,1664]{1,0:T(2,128)S(1)} %add.58), channel_id=1, source_target_pairs={{0,64},{1,65},{2,66},{3,67},{4,68},{5,69},{6,70},{7,71},{8,72},{9,... | collective-permute-start | bytes 39944 | tf_op jit(solution)/shard_map/ppermute | solution.py:43
  163.1 9.4 %collective-permute-start.26 = (f32[2,1664]{1,0:T(2,128)S(1)}, f32[2,1664]{1,0:T(2,128)S(1)}, u32[]{:S(2)}, u32[]{:S(2)}) collective-permute-start(f32[2,1664]{1,0:T(2,128)S(1)} %add.58), channel_id=1, source_target_pairs={{0,192},{1,193},{2,194},{3,195},{4,196},{5,197},{6,198},{7,199},{8... | collective-permute-start | bytes 39944 | tf_op jit(solution)/shard_map/ppermute | solution.py:43
  163.3 13.5 %collective-permute-start.22 = (bf16[192,1664]{1,0:T(8,128)(2,1)S(1)}, bf16[192,1664]{1,0:T(8,128)(2,1)S(1)}, u32[]{:S(2)}, u32[]{:S(2)}) collective-permute-start(bf16[192,1664]{1,0:T(8,128)(2,1)S(1)} %add_convert_fusion.1), channel_id=1, source_target_pairs={{0,64},{32,96},{64,128},{96,160},{128,192},{160,224},{192,0},{224,... | collective-permute-start | bytes 1916936 | tf_op jit(solution)/shard_map/ppermute | solution.py:31
  163.6 13.3 %collective-permute-start.23 = (bf16[192,1664]{1,0:T(8,128)(2,1)S(1)}, bf16[192,1664]{1,0:T(8,128)(2,1)S(1)}, u32[]{:S(2)}, u32[]{:S(2)}) collective-permute-start(bf16[192,1664]{1,0:T(8,128)(2,1)S(1)} %add_convert_fusion.2), channel_id=1, source_target_pairs={{0,32},{32,0},{64,96},{96,64},{128,160},{160,128},{192,224},{224,1... | collective-permute-start | bytes 1916936 | tf_op jit(solution)/shard_map/ppermute | solution.py:39
  165.0 11.9 %collective-permute-start.21 = (bf16[192,1664]{1,0:T(8,128)(2,1)S(1)}, bf16[192,1664]{1,0:T(8,128)(2,1)S(1)}, u32[]{:S(2)}, u32[]{:S(2)}) collective-permute-start(bf16[192,1664]{1,0:T(8,128)(2,1)S(1)} %copy-done.33), channel_id=1, source_target_pairs={{0,192},{32,224},{64,0},{96,32},{128,64},{160,96},{192,128},{224,1... | collective-permute-start | bytes 1916936 | tf_op jit(solution)/shard_map/ppermute | solution.py:35
  179.2 27.7 %all-to-all-start.1 = ((bf16[16,16,1664]{2,1,0:T(8,128)(2,1)}), bf16[16,16,1664]{2,1,0:T(8,128)(2,1)S(1)}, u32[]{:S(2)}, u32[]{:S(2)}) async-start(bf16[16,16,1664]{2,1,0:T(8,128)(2,1)} %bitcast.7), calls=%async_computation.1 | async-start | bytes 1703936 | tf_op jit(solution)/shard_map/all_to_all | solution.py:56
  206.8 11.5 %collective-permute-start.27 = (bf16[256,1664]{1,0:T(8,128)(2,1)S(1)}, bf16[256,1664]{1,0:T(8,128)(2,1)S(1)}, u32[]{:S(2)}, u32[]{:S(2)}) collective-permute-start(bf16[256,1664]{1,0:T(8,128)(2,1)S(1)} %bitcast.17), channel_id=1, source_target_pairs={{0,1},{1,0},{2,3},{3,2},{4,5},{5,4},{6,7},{7,6},{8,9},{9,8},{10,11... | collective-permute-start | bytes 2555912 | tf_op jit(solution)/shard_map/ppermute | solution.py:43
  (32 other events, 559.0 us)
where the time goes:
time: 225 us; the launch traced here: 220 us
  waiting for transfers between devices  66.9 us (30%)
  starting transfers between devices  58.8 us (26%)
  blocking collectives  42.3 us (19%)
  Pallas kernels  33.2 us (15%)
  matrix products  11.9 us (5%)
  local copies, waits for them, and re-layouts  3.6 us (2%)
  other arithmetic  2.3 us (1%)
    all_to_all x1, blocking collectives, chip_exchange(): x = lax.all_to_all(x, 'expert', 0, 0, axis_index_groups=groups, tiled=True)  42.3 us
    pallas_call x3, Pallas kernels, experts_step(): pl.pallas_call(functools.partial(experts_kernel, len(blocks), parts, plac...  24.8 us
    ppermute x6, waiting for transfers between devices, across(): return lax.ppermute(x, 'dp', ACROSS)  20.3 us
    ppermute x8, waiting for transfers between devices, right(): return lax.ppermute(x, 'dp', RIGHT)  17 us
    ppermute x8, waiting for transfers between devices, left(): return lax.ppermute(x, 'dp', LEFT)  16.2 us
    ppermute x8, starting transfers between devices, left(): return lax.ppermute(x, 'dp', LEFT)  15.9 us
    ppermute x6, starting transfers between devices, swapped(): lax.ppermute(x, ('dp', 'expert'), [(i, i ^ mask) for i in range(256)])  14.7 us
    ppermute x8, starting transfers between devices, right(): return lax.ppermute(x, 'dp', RIGHT)  11.7 us
  transfers between devices with their start and end apart: 29, of which 13 were waited for; matrix products, arithmetic and copies ran while one was open for 6% of the time, Pallas kernels for 9%

commit v1 on v0

--- a/solution.py
+++ b/solution.py
@@ -111,7 +111,7 @@
         functools.partial(regroup_kernel, len(pieces)),
         out_shape=[jax.ShapeDtypeStruct((whole, n), bf16) for n in widths],
         scratch_shapes=[pltpu.VMEM((whole, width), bf16)],
-        compiler_params=pltpu.CompilerParams(vmem_limit_bytes=24 * 2**20),
+        compiler_params=pltpu.CompilerParams(vmem_limit_bytes=60 * 2**20),
         cost_estimate=pl.CostEstimate(flops=1, bytes_accessed=1, transcendentals=0),
     )(table, *pieces)
 

time: 225 us -> 229 us (1.018)
  Pallas kernels: 33.2 us -> 37.9 us
    pallas_call x2, Pallas kernels: 1.71 us -> 6.4 us  [regroup(): pl.pallas_call(functools.partial(regroup_kernel, len(pieces)), out_shape=...]
where the time goes in v1:
time: 229 us; the launch traced here: 224 us
  waiting for transfers between devices  67.2 us (29%)
  starting transfers between devices  58.6 us (26%)
  blocking collectives  42.4 us (19%)
  Pallas kernels  37.9 us (17%)
  matrix products  11.9 us (5%)
  local copies, waits for them, and re-layouts  2.43 us (1%)
  other arithmetic  2.3 us (1%)
    all_to_all x1, blocking collectives, chip_exchange(): x = lax.all_to_all(x, 'expert', 0, 0, axis_index_groups=groups, tiled=True)  42.4 us
    pallas_call x3, Pallas kernels, experts_step(): pl.pallas_call(functools.partial(experts_kernel, len(blocks), parts, plac...  24.8 us
    ppermute x6, waiting for transfers between devices, across(): return lax.ppermute(x, 'dp', ACROSS)  20.5 us
    ppermute x8, waiting for transfers between devices, right(): return lax.ppermute(x, 'dp', RIGHT)  17.1 us
    ppermute x8, waiting for transfers between devices, left(): return lax.ppermute(x, 'dp', LEFT)  16.1 us
    ppermute x8, starting transfers between devices, left(): return lax.ppermute(x, 'dp', LEFT)  15.7 us
    ppermute x6, starting transfers between devices, swapped(): lax.ppermute(x, ('dp', 'expert'), [(i, i ^ mask) for i in range(256)])  14.7 us
    ppermute x8, starting transfers between devices, right(): return lax.ppermute(x, 'dp', RIGHT)  11.9 us
  transfers between devices with their start and end apart: 29, of which 13 were waited for; matrix products, arithmetic and copies ran while one was open for 6% of the time, Pallas kernels for 9%

profile of v1, /device:TPU:1, one launch (start us, length us, event | category | flops | bytes accessed | tf_op | source)
XLA Modules:
  0.0 224.1 jit_solution(10043003933750975425)
XLA Ops:
  0.6 3.6 %shard_map.172 = (bf16[192,1664]{1,0:T(8,128)(2,1)}, bf16[192,1664]{1,0:T(8,128)(2,1)}) custom-call(bf16[128,1664]{1,0:T(8,128)(2,1)} %tok.1, bf16[128,1664]{1,0:T(8,128)(2,1)} %cot.1, s32[2,128]{1,0:T(2,128)} %bitcast.17, s32[2,128]{1,0:T(2,128)} %bitcast.19, f32[2,128]{1,0:T(2,128)} %bitcast.29, f32[1664]{0:T(1024)} %gain.1, f32[1664]{0:T(1024)} %shift.1), custom_call_target="tpu_custom_call" | custom-call | tf_op jit(solution)/shard_map/pallas_call | solution.py:292
  4.2 3.3 %collective-permute-start = (bf16[192,1664]{1,0:T(8,128)(2,1)}, bf16[192,1664]{1,0:T(8,128)(2,1)S(1)}, u32[]{:S(2)}, u32[]{:S(2)}) collective-permute-start(bf16[192,1664]{1,0:T(8,128)(2,1)} %get-tuple-element.59), channel_id=1, source_target_pairs={{0,1},{1,0},{2,3},{3,2},{4,5},{5,4},{6,7},{7,6},{8,9},{9,8},{10,11... | collective-permute-start | bytes 1916936 | tf_op jit(solution)/shard_map/ppermute | solution.py:43
  7.6 1.9 collective-permute-done.refs_1_
  10.3 3.3 %shard_map.173 = bf16[384,1664]{1,0:T(8,128)(2,1)} custom-call(bf16[384,384]{1,0:T(8,128)(2,1)} %constant.6.clone.table, bf16[192,1664]{1,0:T(8,128)(2,1)} %get-tuple-element.58.refs_0_, bf16[192,1664]{1,0:T(8,128)(2,1)} %copy-done.18), custom_call_target="tpu_custom_call" | custom-call | flops 1 | bytes 1 | tf_op jit(solution)/shard_map/pallas_call | solution.py:110
  13.6 42.4 %all_to_all.10 = bf16[16,24,1664]{2,1,0:T(8,128)(2,1)} all-to-all(bf16[16,24,1664]{2,1,0:T(8,128)(2,1)} %bitcast.28), channel_id=1, replica_groups={{0,2,4,6,8,10,12,14,16,18,20,22,24,26,28,30},{1,3,5,7,9,11,13,15,17,19,..., dimensions={0} | all-to-all | bytes 2555904 | tf_op jit(solution)/shard_map/all_to_all | solution.py:56
  56.1 3.1 %shard_map.174 = (bf16[384,768]{1,0:T(8,128)(2,1)}, bf16[384,896]{1,0:T(8,128)(2,1)}) custom-call(bf16[384,384]{1,0:T(8,128)(2,1)} %constant.7.clone.table, bf16[384,1664]{1,0:T(8,128)(2,1)} %bitcast.27), custom_call_target="tpu_custom_call" | custom-call | flops 1 | bytes 1 | tf_op jit(solution)/shard_map/pallas_call | solution.py:110
  59.2 2.5 %collective-permute-start.4 = (bf16[384,896]{1,0:T(8,128)(2,1)}, bf16[384,896]{1,0:T(8,128)(2,1)S(1)}, u32[]{:S(2)}, u32[]{:S(2)}) collective-permute-start(bf16[384,896]{1,0:T(8,128)(2,1)} %get-tuple-element.66.refs_7_), channel_id=1, source_target_pairs={{0,192},{32,224},{64,0},{96,32},{128,64},{160,96},{192,128},{224,1... | collective-permute-start | bytes 2064392 | tf_op jit(solution)/shard_map/ppermute | solution.py:35
  64.6 8.8 %collective-permute-done.5.refs_6_ = bf16[384,768]{1,0:T(8,128)(2,1)S(1)} collective-permute-done((bf16[384,768]{1,0:T(8,128)(2,1)}, bf16[384,768]{1,0:T(8,128)(2,1)S(1)}, u32[]{:S(2)}, u32[]{:S(2)}) %collective-permute-start.5) | collective-permute-done | bytes 589856 | tf_op jit(solution)/shard_map/ppermute | solution.py:39
  74.8 11.6 %collective-permute-done.3.refs_5_ = bf16[384,768]{1,0:T(8,128)(2,1)} collective-permute-done((bf16[384,768]{1,0:T(8,128)(2,1)}, bf16[384,768]{1,0:T(8,128)(2,1)}, u32[]{:S(2)}, u32[]{:S(2)}) %collective-permute-start.3) | collective-permute-done | bytes 589856 | tf_op jit(solution)/shard_map/ppermute | solution.py:35
  86.9 2.9 %collective-permute-start.8 = (bf16[384,768]{1,0:T(8,128)(2,1)}, bf16[384,768]{1,0:T(8,128)(2,1)}, u32[]{:S(2)}, u32[]{:S(2)}) collective-permute-start(bf16[384,768]{1,0:T(8,128)(2,1)} %collective-permute-done.3.refs_5_), channel_id=1, source_target_pairs={{0,192},{32,224},{64,0},{96,32},{128,64},{160,96},{192,128},{224,1... | collective-permute-start | bytes 1769480 | tf_op jit(solution)/shard_map/ppermute | solution.py:35
  89.8 1.4 collective-permute-start.11
  91.3 11.7 %collective-permute-done.12.refs_8_ = bf16[384,896]{1,0:T(8,128)(2,1)S(1)} collective-permute-done((bf16[384,896]{1,0:T(8,128)(2,1)S(1)}, bf16[384,896]{1,0:T(8,128)(2,1)S(1)}, u32[]{:S(2)}, u32[]{:S(2)}) %collective-permute-start.12) | collective-permute-done | bytes 688160 | tf_op jit(solution)/shard_map/ppermute | solution.py:39
  105.8 10.5 %shard_map.175 = (bf16[1536,1664]{1,0:T(8,128)(2,1)}, bf16[1536,1664]{1,0:T(8,128)(2,1)}, bf16[1536,512]{1,0:T(8,128)(2,1)}, bf16[1536,512]{1,0:T(8,128)(2,1)}, ...) custom-call(bf16[1664,512]{1,0:T(8,128)(2,1)} %bitcast.21, ...), custom_call_target="tpu_custom_call" | custom-call | flops 1 | bytes 1 | tf_op jit(solution)/shard_map/pallas_call | solution.py:187
  116.4 2.2 collective-permute-done.10.refs_6_
  118.5 8.7 %shard_map.176 = (bf16[1536,1664]{1,0:T(8,128)(2,1)}, bf16[1536,1664]{1,0:T(8,128)(2,1)}, bf16[1536,512]{1,0:T(8,128)(2,1)}, bf16[1536,512]{1,0:T(8,128)(2,1)}, ...) custom-call(bf16[1664,512]{1,0:T(8,128)(2,1)} %bitcast.22, ...), custom_call_target="tpu_custom_call", output_to_operand_aliasing={{0}: (9, {}), {1}: (10, {}), {2}: (11, {}), {3}: (12, {})} | custom-call | flops 1 | bytes 1 | tf_op jit(solution)/shard_map/pallas_call | solution.py:187
  127.3 3.9 %collective-permute-done.13.refs_3_ = bf16[384,768]{1,0:T(8,128)(2,1)} collective-permute-done((bf16[384,768]{1,0:T(8,128)(2,1)}, bf16[384,768]{1,0:T(8,128)(2,1)}, u32[]{:S(2)}, u32[]{:S(2)}) %collective-permute-start.13) | collective-permute-done | bytes 589856 | tf_op jit(solution)/shard_map/ppermute | solution.py:31
  132.1 5.6 %shard_map.177 = (bf16[1536,1664]{1,0:T(8,128)(2,1)}, bf16[1536,1664]{1,0:T(8,128)(2,1)}, bf16[1536,512]{1,0:T(8,128)(2,1)}, bf16[1536,512]{1,0:T(8,128)(2,1)}, ...) custom-call(bf16[1664,512]{1,0:T(8,128)(2,1)} %bitcast.23, ...), custom_call_target="tpu_custom_call", output_to_operand_aliasing={{0}: (5, {}), {1}: (6, {}), {2}: (7, {}), {3}: (8, {})} | custom-call | flops 1 | bytes 1 | tf_op jit(solution)/shard_map/pallas_call | solution.py:187
  139.7 2.6 %collective-permute-start.15 = (bf16[96,1664]{1,0:T(8,128)(2,1)}, bf16[96,1664]{1,0:T(8,128)(2,1)S(1)}, u32[]{:S(2)}, u32[]{:S(2)}) collective-permute-start(bf16[96,1664]{1,0:T(8,128)(2,1)} %get-tuple-element.82), channel_id=1, source_target_pairs={{0,192},{32,224},{64,0},{96,32},{128,64},{160,96},{192,128},{224,1... | collective-permute-start | bytes 958472 | tf_op jit(solution)/shard_map/ppermute | solution.py:35
  142.3 2.7 %collective-permute-done.17 = bf16[96,1664]{1,0:T(8,128)(2,1)S(1)} collective-permute-done((bf16[96,1664]{1,0:T(8,128)(2,1)}, bf16[96,1664]{1,0:T(8,128)(2,1)S(1)}, u32[]{:S(2)}, u32[]{:S(2)}) %collective-permute-start.17) | collective-permute-done | bytes 319520 | tf_op jit(solution)/shard_map/ppermute | solution.py:31
  145.0 9.4 %collective-permute-start.19 = (bf16[192,1664]{1,0:T(8,128)(2,1)S(1)}, bf16[192,1664]{1,0:T(8,128)(2,1)S(1)}, u32[]{:S(2)}, u32[]{:S(2)}) collective-permute-start(bf16[192,1664]{1,0:T(8,128)(2,1)S(1)} %copy-done.32), channel_id=1, source_target_pairs={{0,64},{32,96},{64,128},{96,160},{128,192},{160,224},{192,0},{224,... | collective-permute-start | bytes 1916936 | tf_op jit(solution)/shard_map/ppermute | solution.py:31
  155.9 2.7 %collective-permute-start.16 = (bf16[192,1664]{1,0:T(8,128)(2,1)S(1)}, bf16[192,1664]{1,0:T(8,128)(2,1)S(1)}, u32[]{:S(2)}, u32[]{:S(2)}) collective-permute-start(bf16[192,1664]{1,0:T(8,128)(2,1)S(1)} %pad_maximum_fusion), channel_id=1, source_target_pairs={{0,192},{32,224},{64,0},{96,32},{128,64},{160,96},{192,128},{224,1... | collective-permute-start | bytes 1916936 | tf_op jit(solution)/shard_map/ppermute | solution.py:35
  159.3 7.7 %collective-permute-done.19 = bf16[192,1664]{1,0:T(8,128)(2,1)S(1)} collective-permute-done((bf16[192,1664]{1,0:T(8,128)(2,1)S(1)}, bf16[192,1664]{1,0:T(8,128)(2,1)S(1)}, u32[]{:S(2)}, u32[]{:S(2)}) %collective-permute-start.19) | collective-permute-done | bytes 639008 | tf_op jit(solution)/shard_map/ppermute | solution.py:31
  168.8 3.0 %collective-permute-start.21 = (bf16[192,1664]{1,0:T(8,128)(2,1)S(1)}, bf16[192,1664]{1,0:T(8,128)(2,1)S(1)}, u32[]{:S(2)}, u32[]{:S(2)}) collective-permute-start(bf16[192,1664]{1,0:T(8,128)(2,1)S(1)} %copy-done.31), channel_id=1, source_target_pairs={{0,192},{32,224},{64,0},{96,32},{128,64},{160,96},{192,128},{224,1... | collective-permute-start | bytes 1916936 | tf_op jit(solution)/shard_map/ppermute | solution.py:35
  171.8 4.6 %fusion = f32[1664,512]{1,0:T(8,128)} fusion(bf16[1536,1664]{1,0:T(8,128)(2,1)S(1)} %copy-done.7, bf16[1536,512]{1,0:T(8,128)(2,1)S(1)} %copy-done.9), kind=kOutput, calls=%fused_computation.10 | convolution fusion | flops 2617245696 | bytes 10092544 | tf_op jit(solution)/shard_map/dot_general | solution.py:342
  176.4 4.3 %collective-permute-done.21 = bf16[192,1664]{1,0:T(8,128)(2,1)S(1)} collective-permute-done((bf16[192,1664]{1,0:T(8,128)(2,1)S(1)}, bf16[192,1664]{1,0:T(8,128)(2,1)S(1)}, u32[]{:S(2)}, u32[]{:S(2)}) %collective-permute-start.21) | collective-permute-done | bytes 639008 | tf_op jit(solution)/shard_map/ppermute | solution.py:35
  181.6 1.3 shard_map.178
  183.0 10.1 %all-to-all-start.1 = ((bf16[16,16,1664]{2,1,0:T(8,128)(2,1)}), bf16[16,16,1664]{2,1,0:T(8,128)(2,1)S(1)}, u32[]{:S(2)}, u32[]{:S(2)}) async-start(bf16[16,16,1664]{2,1,0:T(8,128)(2,1)} %bitcast.7), calls=%async_computation.1 | async-start | bytes 1703936 | tf_op jit(solution)/shard_map/all_to_all | solution.py:56
  193.2 7.3 %fusion.1 = f32[512,1664]{1,0:T(8,128)} fusion(bf16[1536,512]{1,0:T(8,128)(2,1)S(1)} %copy-done.8, bf16[1536,1664]{1,0:T(8,128)(2,1)} %get-tuple-element.100), kind=kOutput, calls=%fused_computation.11 | convolution fusion | flops 2617245696 | bytes 10092544 | tf_op jit(solution)/shard_map/dot_general | solution.py:343
  200.5 10.1 %all-to-all-done.1 = bf16[16,16,1664]{2,1,0:T(8,128)(2,1)S(1)} async-done(((bf16[16,16,1664]{2,1,0:T(8,128)(2,1)}), bf16[16,16,1664]{2,1,0:T(8,128)(2,1)S(1)}, u32[]{:S(2)}, u32[]{:S(2)}) %all-to-all-start.1) | async-done | bytes 852000 | tf_op jit(solution)/shard_map/all_to_all | solution.py:56
  210.6 9.5 %collective-permute-start.27 = (bf16[256,1664]{1,0:T(8,128)(2,1)S(1)}, bf16[256,1664]{1,0:T(8,128)(2,1)S(1)}, u32[]{:S(2)}, u32[]{:S(2)}) collective-permute-start(bf16[256,1664]{1,0:T(8,128)(2,1)S(1)} %bitcast.15), channel_id=1, source_target_pairs={{0,1},{1,0},{2,3},{3,2},{4,5},{5,4},{6,7},{7,6},{8,9},{9,8},{10,11... | collective-permute-start | bytes 2555912 | tf_op jit(solution)/shard_map/ppermute | solution.py:43
  220.7 1.4 collective-permute-done.27.far
  222.2 1.7 shard_map.179
  (114 shorter events, 17.0 us)
Async XLA Ops:
  4.2 5.2 %collective-permute-start = (bf16[192,1664]{1,0:T(8,128)(2,1)}, bf16[192,1664]{1,0:T(8,128)(2,1)S(1)}, u32[]{:S(2)}, u32[]{:S(2)}) collective-permute-start(bf16[192,1664]{1,0:T(8,128)(2,1)} %get-tuple-element.59), channel_id=1, source_target_pairs={{0,1},{1,0},{2,3},{3,2},{4,5},{5,4},{6,7},{7,6},{8,9},{9,8},{10,11... | collective-permute-start | bytes 1916936 | tf_op jit(solution)/shard_map/ppermute | solution.py:43
  59.2 14.5 %collective-permute-start.4 = (bf16[384,896]{1,0:T(8,128)(2,1)}, bf16[384,896]{1,0:T(8,128)(2,1)S(1)}, u32[]{:S(2)}, u32[]{:S(2)}) collective-permute-start(bf16[384,896]{1,0:T(8,128)(2,1)} %get-tuple-element.66.refs_7_), channel_id=1, source_target_pairs={{0,192},{32,224},{64,0},{96,32},{128,64},{160,96},{192,128},{224,1... | collective-permute-start | bytes 2064392 | tf_op jit(solution)/shard_map/ppermute | solution.py:35
  61.7 11.7 %collective-permute-start.5 = (bf16[384,768]{1,0:T(8,128)(2,1)}, bf16[384,768]{1,0:T(8,128)(2,1)S(1)}, u32[]{:S(2)}, u32[]{:S(2)}) collective-permute-start(bf16[384,768]{1,0:T(8,128)(2,1)} %get-tuple-element.62.refs_3_), channel_id=1, source_target_pairs={{0,32},{32,0},{64,96},{96,64},{128,160},{160,128},{192,224},{224,1... | collective-permute-start | bytes 1769480 | tf_op jit(solution)/shard_map/ppermute | solution.py:39
  62.1 24.2 %collective-permute-start.3 = (bf16[384,768]{1,0:T(8,128)(2,1)}, bf16[384,768]{1,0:T(8,128)(2,1)}, u32[]{:S(2)}, u32[]{:S(2)}) collective-permute-start(bf16[384,768]{1,0:T(8,128)(2,1)} %get-tuple-element.62.refs_3_), channel_id=1, source_target_pairs={{0,192},{32,224},{64,0},{96,32},{128,64},{160,96},{192,128},{224,1... | collective-permute-start | bytes 1769480 | tf_op jit(solution)/shard_map/ppermute | solution.py:35
  62.5 24.4 %collective-permute-start.1 = (bf16[384,768]{1,0:T(8,128)(2,1)}, bf16[384,768]{1,0:T(8,128)(2,1)S(1)}, u32[]{:S(2)}, u32[]{:S(2)}) collective-permute-start(bf16[384,768]{1,0:T(8,128)(2,1)} %get-tuple-element.62.refs_3_), channel_id=1, source_target_pairs={{0,64},{32,96},{64,128},{96,160},{128,192},{160,224},{192,0},{224,... | collective-permute-start | bytes 1769480 | tf_op jit(solution)/shard_map/ppermute | solution.py:31
  63.6 26.2 %collective-permute-start.6 = (bf16[384,896]{1,0:T(8,128)(2,1)}, bf16[384,896]{1,0:T(8,128)(2,1)S(1)}, u32[]{:S(2)}, u32[]{:S(2)}) collective-permute-start(bf16[384,896]{1,0:T(8,128)(2,1)} %get-tuple-element.66.refs_7_), channel_id=1, source_target_pairs={{0,32},{32,0},{64,96},{96,64},{128,160},{160,128},{192,224},{224,1... | collective-permute-start | bytes 2064392 | tf_op jit(solution)/shard_map/ppermute | solution.py:39
  73.4 29.6 %copy-start.20 = (bf16[384,768]{1,0:T(8,128)(2,1)}, bf16[384,768]{1,0:T(8,128)(2,1)S(1)}, u32[]{:S(2)}) copy-start(bf16[384,768]{1,0:T(8,128)(2,1)S(1)} %collective-permute-done.5.refs_6_) | copy-start | bytes 1769476
  73.4 17.8 %collective-permute-start.2 = (bf16[384,896]{1,0:T(8,128)(2,1)}, bf16[384,896]{1,0:T(8,128)(2,1)S(1)}, u32[]{:S(2)}, u32[]{:S(2)}) collective-permute-start(bf16[384,896]{1,0:T(8,128)(2,1)} %get-tuple-element.66.refs_7_), channel_id=1, source_target_pairs={{0,64},{32,96},{64,128},{96,160},{128,192},{160,224},{192,0},{224,... | collective-permute-start | bytes 2064392 | tf_op jit(solution)/shard_map/ppermute | solution.py:31
  73.7 32.1 %copy-start.11 = (bf16[384,896]{1,0:T(8,128)(2,1)}, bf16[384,896]{1,0:T(8,128)(2,1)S(1)}, u32[]{:S(2)}) copy-start(bf16[384,896]{1,0:T(8,128)(2,1)S(1)} %collective-permute-done.4.refs_9_) | copy-start | bytes 2064388
  73.7 29.3 %collective-permute-start.12 = (bf16[384,896]{1,0:T(8,128)(2,1)S(1)}, bf16[384,896]{1,0:T(8,128)(2,1)S(1)}, u32[]{:S(2)}, u32[]{:S(2)}) collective-permute-start(bf16[384,896]{1,0:T(8,128)(2,1)S(1)} %collective-permute-done.4.refs_9_), channel_id=1, source_target_pairs={{0,32},{32,0},{64,96},{96,64},{128,160},{160,128},{192,224},{224,1... | collective-permute-start | bytes 2064392 | tf_op jit(solution)/shard_map/ppermute | solution.py:39
  86.3 17.5 %collective-permute-start.7 = (bf16[384,768]{1,0:T(8,128)(2,1)S(1)}, bf16[384,768]{1,0:T(8,128)(2,1)}, u32[]{:S(2)}, u32[]{:S(2)}) collective-permute-start(bf16[384,768]{1,0:T(8,128)(2,1)S(1)} %collective-permute-done.5.refs_6_), channel_id=1, source_target_pairs={{0,64},{32,96},{64,128},{96,160},{128,192},{160,224},{192,0},{224,... | collective-permute-start | bytes 1769480 | tf_op jit(solution)/shard_map/ppermute | solution.py:31
  86.9 18.2 %collective-permute-start.8 = (bf16[384,768]{1,0:T(8,128)(2,1)}, bf16[384,768]{1,0:T(8,128)(2,1)}, u32[]{:S(2)}, u32[]{:S(2)}) collective-permute-start(bf16[384,768]{1,0:T(8,128)(2,1)} %collective-permute-done.3.refs_5_), channel_id=1, source_target_pairs={{0,192},{32,224},{64,0},{96,32},{128,64},{160,96},{192,128},{224,1... | collective-permute-start | bytes 1769480 | tf_op jit(solution)/shard_map/ppermute | solution.py:35
  89.8 26.5 %collective-permute-start.11 = (bf16[384,896]{1,0:T(8,128)(2,1)S(1)}, bf16[384,896]{1,0:T(8,128)(2,1)S(1)}, u32[]{:S(2)}, u32[]{:S(2)}) collective-permute-start(bf16[384,896]{1,0:T(8,128)(2,1)S(1)} %collective-permute-done.4.refs_9_), channel_id=1, source_target_pairs={{0,192},{32,224},{64,0},{96,32},{128,64},{160,96},{192,128},{224,1... | collective-permute-start | bytes 2064392 | tf_op jit(solution)/shard_map/ppermute | solution.py:35
  91.2 27.3 %collective-permute-start.10 = (bf16[384,896]{1,0:T(8,128)(2,1)S(1)}, bf16[384,896]{1,0:T(8,128)(2,1)}, u32[]{:S(2)}, u32[]{:S(2)}) collective-permute-start(bf16[384,896]{1,0:T(8,128)(2,1)S(1)} %collective-permute-done.6.refs_10_), channel_id=1, source_target_pairs={{0,64},{32,96},{64,128},{96,160},{128,192},{160,224},{192,0},{224,... | collective-permute-start | bytes 2064392 | tf_op jit(solution)/shard_map/ppermute | solution.py:31
  103.0 28.2 %collective-permute-start.14 = (bf16[384,896]{1,0:T(8,128)(2,1)S(1)}, bf16[384,896]{1,0:T(8,128)(2,1)S(1)}, u32[]{:S(2)}, u32[]{:S(2)}) collective-permute-start(bf16[384,896]{1,0:T(8,128)(2,1)S(1)} %collective-permute-done.12.refs_8_), channel_id=1, source_target_pairs={{0,192},{32,224},{64,0},{96,32},{128,64},{160,96},{192,128},{224,1... | collective-permute-start | bytes 2064392 | tf_op jit(solution)/shard_map/ppermute | solution.py:35
  103.8 12.5 %collective-permute-start.9 = (bf16[384,768]{1,0:T(8,128)(2,1)}, bf16[384,768]{1,0:T(8,128)(2,1)}, u32[]{:S(2)}, u32[]{:S(2)}) collective-permute-start(bf16[384,768]{1,0:T(8,128)(2,1)} %collective-permute-done.3.refs_5_), channel_id=1, source_target_pairs={{0,32},{32,0},{64,96},{96,64},{128,160},{160,128},{192,224},{224,1... | collective-permute-start | bytes 1769480 | tf_op jit(solution)/shard_map/ppermute | solution.py:39
  105.1 26.1 %collective-permute-start.13 = (bf16[384,768]{1,0:T(8,128)(2,1)}, bf16[384,768]{1,0:T(8,128)(2,1)}, u32[]{:S(2)}, u32[]{:S(2)}) collective-permute-start(bf16[384,768]{1,0:T(8,128)(2,1)} %collective-permute-done.7.refs_3_), channel_id=1, source_target_pairs={{0,64},{32,96},{64,128},{96,160},{128,192},{160,224},{192,0},{224,... | collective-permute-start | bytes 1769480 | tf_op jit(solution)/shard_map/ppermute | solution.py:31
  132.0 36.8 %copy-start.31 = (bf16[192,1664]{1,0:T(8,128)(2,1)S(1)}, bf16[192,1664]{1,0:T(8,128)(2,1)}, u32[]{:S(2)}) copy-start(bf16[192,1664]{1,0:T(8,128)(2,1)} %get-tuple-element.94) | copy-start | bytes 1916932
  137.7 7.3 %collective-permute-start.17 = (bf16[96,1664]{1,0:T(8,128)(2,1)}, bf16[96,1664]{1,0:T(8,128)(2,1)S(1)}, u32[]{:S(2)}, u32[]{:S(2)}) collective-permute-start(bf16[96,1664]{1,0:T(8,128)(2,1)} %get-tuple-element.86), channel_id=1, source_target_pairs={{0,64},{32,96},{64,128},{96,160},{128,192},{160,224},{192,0},{224,... | collective-permute-start | bytes 958472 | tf_op jit(solution)/shard_map/ppermute | solution.py:31
  138.5 3.8 %collective-permute-start.18 = (f32[2,1664]{1,0:T(2,128)S(1)}, f32[2,1664]{1,0:T(2,128)S(1)}, u32[]{:S(2)}, u32[]{:S(2)}) collective-permute-start(f32[2,1664]{1,0:T(2,128)S(1)} %add_add_fusion.1), channel_id=1, source_target_pairs={{0,32},{1,33},{2,34},{3,35},{4,36},{5,37},{6,38},{7,39},{8,40},{9,... | collective-permute-start | bytes 39944 | tf_op jit(solution)/shard_map/ppermute | solution.py:43
  139.7 16.1 %collective-permute-start.15 = (bf16[96,1664]{1,0:T(8,128)(2,1)}, bf16[96,1664]{1,0:T(8,128)(2,1)S(1)}, u32[]{:S(2)}, u32[]{:S(2)}) collective-permute-start(bf16[96,1664]{1,0:T(8,128)(2,1)} %get-tuple-element.82), channel_id=1, source_target_pairs={{0,192},{32,224},{64,0},{96,32},{128,64},{160,96},{192,128},{224,1... | collective-permute-start | bytes 958472 | tf_op jit(solution)/shard_map/ppermute | solution.py:35
  145.0 22.0 %collective-permute-start.19 = (bf16[192,1664]{1,0:T(8,128)(2,1)S(1)}, bf16[192,1664]{1,0:T(8,128)(2,1)S(1)}, u32[]{:S(2)}, u32[]{:S(2)}) collective-permute-start(bf16[192,1664]{1,0:T(8,128)(2,1)S(1)} %copy-done.32), channel_id=1, source_target_pairs={{0,64},{32,96},{64,128},{96,160},{128,192},{160,224},{192,0},{224,... | collective-permute-start | bytes 1916936 | tf_op jit(solution)/shard_map/ppermute | solution.py:31
  154.6 12.5 %collective-permute-start.20 = (bf16[192,1664]{1,0:T(8,128)(2,1)S(1)}, bf16[192,1664]{1,0:T(8,128)(2,1)S(1)}, u32[]{:S(2)}, u32[]{:S(2)}) collective-permute-start(bf16[192,1664]{1,0:T(8,128)(2,1)S(1)} %pad_maximum_fusion.1), channel_id=1, source_target_pairs={{0,32},{32,0},{64,96},{96,64},{128,160},{160,128},{192,224},{224,1... | collective-permute-start | bytes 1916936 | tf_op jit(solution)/shard_map/ppermute | solution.py:39
  155.9 11.5 %collective-permute-start.16 = (bf16[192,1664]{1,0:T(8,128)(2,1)S(1)}, bf16[192,1664]{1,0:T(8,128)(2,1)S(1)}, u32[]{:S(2)}, u32[]{:S(2)}) collective-permute-start(bf16[192,1664]{1,0:T(8,128)(2,1)S(1)} %pad_maximum_fusion), channel_id=1, source_target_pairs={{0,192},{32,224},{64,0},{96,32},{128,64},{160,96},{192,128},{224,1... | collective-permute-start | bytes 1916936 | tf_op jit(solution)/shard_map/ppermute | solution.py:35
  158.6 10.2 %collective-permute-start.24 = (f32[2,1664]{1,0:T(2,128)S(1)}, f32[2,1664]{1,0:T(2,128)S(1)}, u32[]{:S(2)}, u32[]{:S(2)}) collective-permute-start(f32[2,1664]{1,0:T(2,128)S(1)} %add.58), channel_id=1, source_target_pairs={{0,128},{1,129},{2,130},{3,131},{4,132},{5,133},{6,134},{7,135},{8... | collective-permute-start | bytes 39944 | tf_op jit(solution)/shard_map/ppermute | solution.py:43
  158.7 17.7 %collective-permute-start.25 = (f32[2,1664]{1,0:T(2,128)S(1)}, f32[2,1664]{1,0:T(2,128)S(1)}, u32[]{:S(2)}, u32[]{:S(2)}) collective-permute-start(f32[2,1664]{1,0:T(2,128)S(1)} %add.58), channel_id=1, source_target_pairs={{0,64},{1,65},{2,66},{3,67},{4,68},{5,69},{6,70},{7,71},{8,72},{9,... | collective-permute-start | bytes 39944 | tf_op jit(solution)/shard_map/ppermute | solution.py:43
  167.0 9.4 %collective-permute-start.26 = (f32[2,1664]{1,0:T(2,128)S(1)}, f32[2,1664]{1,0:T(2,128)S(1)}, u32[]{:S(2)}, u32[]{:S(2)}) collective-permute-start(f32[2,1664]{1,0:T(2,128)S(1)} %add.58), channel_id=1, source_target_pairs={{0,192},{1,193},{2,194},{3,195},{4,196},{5,197},{6,198},{7,199},{8... | collective-permute-start | bytes 39944 | tf_op jit(solution)/shard_map/ppermute | solution.py:43
  167.3 13.4 %collective-permute-start.22 = (bf16[192,1664]{1,0:T(8,128)(2,1)S(1)}, bf16[192,1664]{1,0:T(8,128)(2,1)S(1)}, u32[]{:S(2)}, u32[]{:S(2)}) collective-permute-start(bf16[192,1664]{1,0:T(8,128)(2,1)S(1)} %add_convert_fusion.1), channel_id=1, source_target_pairs={{0,64},{32,96},{64,128},{96,160},{128,192},{160,224},{192,0},{224,... | collective-permute-start | bytes 1916936 | tf_op jit(solution)/shard_map/ppermute | solution.py:31
  167.5 13.2 %collective-permute-start.23 = (bf16[192,1664]{1,0:T(8,128)(2,1)S(1)}, bf16[192,1664]{1,0:T(8,128)(2,1)S(1)}, u32[]{:S(2)}, u32[]{:S(2)}) collective-permute-start(bf16[192,1664]{1,0:T(8,128)(2,1)S(1)} %add_convert_fusion.2), channel_id=1, source_target_pairs={{0,32},{32,0},{64,96},{96,64},{128,160},{160,128},{192,224},{224,1... | collective-permute-start | bytes 1916936 | tf_op jit(solution)/shard_map/ppermute | solution.py:39
  168.8 11.9 %collective-permute-start.21 = (bf16[192,1664]{1,0:T(8,128)(2,1)S(1)}, bf16[192,1664]{1,0:T(8,128)(2,1)S(1)}, u32[]{:S(2)}, u32[]{:S(2)}) collective-permute-start(bf16[192,1664]{1,0:T(8,128)(2,1)S(1)} %copy-done.31), channel_id=1, source_target_pairs={{0,192},{32,224},{64,0},{96,32},{128,64},{160,96},{192,128},{224,1... | collective-permute-start | bytes 1916936 | tf_op jit(solution)/shard_map/ppermute | solution.py:35
  183.0 27.7 %all-to-all-start.1 = ((bf16[16,16,1664]{2,1,0:T(8,128)(2,1)}), bf16[16,16,1664]{2,1,0:T(8,128)(2,1)S(1)}, u32[]{:S(2)}, u32[]{:S(2)}) async-start(bf16[16,16,1664]{2,1,0:T(8,128)(2,1)} %bitcast.7), calls=%async_computation.1 | async-start | bytes 1703936 | tf_op jit(solution)/shard_map/all_to_all | solution.py:56
  210.6 11.5 %collective-permute-start.27 = (bf16[256,1664]{1,0:T(8,128)(2,1)S(1)}, bf16[256,1664]{1,0:T(8,128)(2,1)S(1)}, u32[]{:S(2)}, u32[]{:S(2)}) collective-permute-start(bf16[256,1664]{1,0:T(8,128)(2,1)S(1)} %bitcast.15), channel_id=1, source_target_pairs={{0,1},{1,0},{2,3},{3,2},{4,5},{5,4},{6,7},{7,6},{8,9},{9,8},{10,11... | collective-permute-start | bytes 2555912 | tf_op jit(solution)/shard_map/ppermute | solution.py:43
  (30 other events, 487.6 us)
